TPU v7x, 256 devices: a whole 4x4x8 slice. The times are simulated.
256 devices in a mesh: ctx: 16 (over x, y_hi, core), tp: 16 (over y_lo, z).
Axes of the slice: x: 4, y: 4 (y_hi: 2, y_lo: 2; y = y_hi * 2 + y_lo), z: 8, core: 2. Of those that a mesh axis runs over, the one named last changes fastest.
Arguments:
- c_query: bfloat16 [4096, 1536], P('ctx'), may hold values from -6 to 6
- w_uq: bfloat16 [1536, 12288], P(None, 'tp'), may hold values from -0.15625 to 0.15625
- w_uk: bfloat16 [64, 128, 512], P('tp'), may hold values from -0.5 to 0.5
- w_uv: bfloat16 [64, 512, 128], P('tp'), may hold values from -0.25 to 0.25
- w_out: bfloat16 [8192, 7168], P('tp'), may hold values from -0.09375 to 0.09375
- kv_latent: bfloat16 [4096, 576], P('ctx'), may hold values from -48 to 48
- slab_order: int32 [32], replicated, may hold values from 0 to 31, each once
- block_table: int32 [32, 32], replicated, may hold values from 0 to 1, as said below
Outputs:
- attn_out: bfloat16 [4096, 7168], P('ctx', 'tp')
Inputs may be any that keep to these rules, and one draw needn't show every extreme that they name: `slab_order`: each of the 32 slabs appears once. `block_table`: entries are 0 or 1, the diagonal is 1.
All inputs are finite; a program needn't handle non-finite values.
Results may differ from a plain program's by a relative error of at most 0.025.
Values may be sent and summed in bfloat16 or wider, within the bound.
A program may use at most 128 MiB of HBM per device.

v0:
```python
import jax
import jax.numpy as jnp
from jax import lax
from jax.sharding import PartitionSpec as P

SLAB = 128


negative_fill = -1e30


def rotate_pairs(values, angles_base):
    half = values.shape[-1] // 2
    freqs = 10000.0 ** (-jnp.arange(half, dtype=jnp.float32) / half)
    angles = angles_base[:, None] * freqs[None, :]
    cosine = jnp.cos(angles)[:, None, :]
    sine = jnp.sin(angles)[:, None, :]
    first = values[..., :half]
    second = values[..., half:]
    return jnp.concatenate(
        [first * cosine - second * sine, second * cosine + first * sine], axis=-1
    )


def slab_lookup(rows, slab_order):
    slab_count = slab_order.shape[0]
    matches = (rows // SLAB)[:, None] == jnp.arange(slab_count, dtype=jnp.int32)[None, :]
    return jnp.sum(jnp.where(matches, slab_order[None, :], 0), axis=1)


def shards(c_query, w_uq, w_uk, w_uv, w_out, kv_latent, slab_order, block_table):
    tok = c_query.shape[0]
    heads_here = w_uk.shape[0]
    nope = w_uk.shape[1]
    lat = w_uk.shape[2]
    rope_dim = kv_latent.shape[1] - lat
    slab_count = slab_order.shape[0]
    scale = (nope + rope_dim) ** (-0.5)
    query = jnp.dot(c_query, w_uq, preferred_element_type=jnp.float32).reshape(
        tok, heads_here, nope + rope_dim
    )
    q_nope = query[..., :nope].astype(jnp.bfloat16)
    q_lat = jnp.einsum("thn,hnl->htl", q_nope, w_uk, preferred_element_type=jnp.float32).astype(
        jnp.bfloat16
    )
    rows = lax.axis_index("ctx") * tok + jnp.arange(tok, dtype=jnp.int32)
    seq_q = slab_lookup(rows, slab_order)
    pos_q = seq_q * SLAB + rows % SLAB
    q_rot = rotate_pairs(query[..., nope:], pos_q.astype(jnp.float32)).astype(jnp.bfloat16)
    q_rot = jnp.transpose(q_rot, (1, 0, 2))
    merged = jnp.concatenate([q_lat, q_rot], axis=-1).reshape(heads_here * tok, lat + rope_dim)
    slab_ids = jnp.arange(slab_count, dtype=jnp.int32)
    seq_onehot = (seq_q[:, None] == slab_ids[None, :]).astype(jnp.float32)
    table_rows = jnp.dot(
        seq_onehot, block_table.astype(jnp.float32), preferred_element_type=jnp.float32
    )
    piece = lax.all_gather(kv_latent, "ctx", axis=0, tiled=True)
    count = piece.shape[0]
    key_rows = jnp.arange(count, dtype=jnp.int32)
    seq_k = slab_lookup(key_rows, slab_order)
    pos_k = seq_k * SLAB + key_rows % SLAB
    key_onehot = (seq_k[:, None] == slab_ids[None, :]).astype(jnp.float32)
    allowed = (
        lax.dot_general(
            table_rows, key_onehot, (((1,), (1,)), ((), ())), preferred_element_type=jnp.float32
        )
        > 0.5
    )
    visible = allowed & (pos_k[None, :] <= pos_q[:, None])
    top_old = jnp.full((heads_here, tok), negative_fill, jnp.float32)
    count = piece.shape[0]
    score = lax.dot_general(
        merged, piece, (((1,), (1,)), ((), ())), preferred_element_type=jnp.float32
    )
    score = score.reshape(heads_here, tok, count) * scale
    score = jnp.where(visible[None, :, :], score, negative_fill)
    top_new = jnp.maximum(top_old, jnp.max(score, axis=-1))
    expo = jnp.exp(score - top_new[..., None])
    total_new = jnp.sum(expo, axis=-1)
    values = jnp.einsum(
        "htj,jl->htl", expo.astype(jnp.bfloat16), piece[:, :lat], preferred_element_type=jnp.float32
    )
    o_lat = (values / total_new[..., None]).astype(jnp.bfloat16)
    o_head = jnp.einsum("htl,hlv->thv", o_lat, w_uv, preferred_element_type=jnp.float32).astype(
        jnp.bfloat16
    )
    o_head = o_head.reshape(tok, heads_here * w_uv.shape[2])
    partial_out = jnp.dot(o_head, w_out, preferred_element_type=jnp.float32)
    return lax.psum_scatter(partial_out.astype(jnp.bfloat16), "tp", scatter_dimension=1, tiled=True)


def solution(mesh):
    in_specs = (
        P("ctx", None),
        P(None, "tp"),
        P("tp", None, None),
        P("tp", None, None),
        P("tp", None),
        P("ctx", None),
        P(),
        P(),
    )
    out_specs = P("ctx", "tp")
    return jax.shard_map(shards, mesh=mesh, in_specs=in_specs, out_specs=out_specs, check_vma=False)
```

profile of v0, /device:TPU:8, one launch (start us, length us, event | category | flops | bytes accessed | tf_op | source)
XLA Modules:
  0.0 204.0 jit_solution(1017209686699223175)
XLA Ops:
  6.5 0.0 copy-start
  6.5 0.0 copy-start.3
  6.5 0.0 all-gather.2.cloned.1.call-start
  6.5 0.7 all-gather.2.cloned.1.call-update
  7.3 0.0 reduce-scatter.2.cloned.1.call-start
  7.3 0.9 copy-done
  8.2 2.2 %fusion.44 = f32[256,768]{0,1:T(8,128)S(1)} fusion(bf16[256,1536]{1,0:T(8,128)(2,1)} %param.8, bf16[1536,768]{1,0:T(8,128)(2,1)S(1)} %copy-done), kind=kOutput, calls=%fused_computation.66 | convolution fusion | flops 603979776 | bytes 3932160 | tf_op jit(solution)/shard_map/dot_general | solution.py:39
  10.4 0.0 copy-start.2
  10.4 0.9 copy-done.2
  11.3 0.2 copy.42
  11.5 0.2 copy.41
  11.7 0.0 copy-start.4
  11.8 0.0 copy-done.3
  11.8 0.1 select_reduce_fusion.1
  11.9 0.5 multiply_cosine_fusion
  12.4 0.1 subtract_convert_fusion
  12.6 0.8 maximum_bitcast_fusion
  13.4 0.2 select_reduce_fusion
  13.6 2.7 %convolution_convert_fusion.1 = bf16[4,256,512]{2,1,0:T(8,128)(2,1)} fusion(bf16[4,128,512]{2,1,0:T(8,128)(2,1)} %param.10, f32[256,4,192]{0,2,1:T(8,128)} %bitcast.25), kind=kOutput, calls=%fused_computation.17 | convolution fusion | flops 134742016 | bytes 1835008 | tf_op jit(solution)/shard_map/thn,hnl->htl/dot_general | solution.py:43
  16.2 0.0 copy-done.4
  16.2 1.3 fusion.11
  17.6 61.0 %all-gather.2.cloned.1.call-done = bf16[4096,576]{0,1:T(8,128)(2,1)} async-done(((bf16[256,576]{0,1:T(8,128)(2,1)}), bf16[4096,576]{0,1:T(8,128)(2,1)}) %all-gather.2.cloned.1.call-update) | async-done | bytes 4718608 | tf_op jit(solution)/shard_map/all_gather | solution.py:57
  78.6 10.1 %fusion = (f32[4,256]{1,0:T(4,128)S(1)}, f32[4,256,4096]{2,1,0:T(8,128)S(1)}) fusion(pred[256,4096]{1,0:T(8,128)(4,1)S(1)} %fusion.11, bf16[4096,576]{0,1:T(8,128)(2,1)} %all-gather.2.cloned.1.call-done, bf16[4,256,64]{2,1,0:T(8,128)(2,1)} %maximum_bitcast_fusion, bf16[4,256,512]{2,1,0:T(8,128)(2,1)} %convolution_convert_fusion.1), kind=kOutput, calls=%fused_computation.2 | convolution fusion | flops 4846779392 | bytes 23728128 | tf_op jit(solution)/shard_map/dot_general | solution.py:72
  88.8 0.0 copy-start.1
  88.8 5.7 %copy-done.1 = f32[4,256,4096]{2,1,0:T(8,128)} copy-done((f32[4,256,4096]{2,1,0:T(8,128)}, f32[4,256,4096]{2,1,0:T(8,128)S(1)}, u32[]{:S(2)}) %copy-start.1) | copy-done | bytes 16777240
  94.5 4.5 %fusion.1 = f32[4,256]{1,0:T(4,128)S(1)} fusion(f32[4,256,4096]{2,1,0:T(8,128)S(1)} %get-tuple-element.14, f32[4,256]{1,0:T(4,128)S(1)} %broadcast_maximum_fusion, pred[256,4096]{1,0:T(8,128)(4,1)S(1)} %fusion.11), kind=kLoop, calls=%fused_computation.3 | loop fusion | flops 16776192 | bytes 17833984 | tf_op jit(solution)/shard_map/reduce_sum | solution.py:79
  99.0 12.8 %convolution_convert_fusion.2 = bf16[4,256,128]{1,2,0:T(8,128)(2,1)} fusion(bf16[4,512,128]{2,1,0:T(8,128)(2,1)} %param.11, f32[4,256]{1,0:T(4,128)S(1)} %fusion.1, f32[4,256,4096]{2,1,0:T(8,128)} %copy-done.1, f32[4,256]{1,0:T(4,128)S(1)} %broadcast_maximum_fusion, pred[256,4096]{1,0:T(8,128)(4,1)S(1)} %fusion.11, ...), kind=kOutput, calls=%fused_computation.21 | convolution fusion | flops 4447141888 | bytes 22814720 | tf_op jit(solution)/shard_map/htl,hlv->thv/dot_general | solution.py:84
  111.8 7.9 %convolution_convert_fusion = bf16[256,7168]{0,1:T(8,128)(2,1)} fusion(bf16[256,512]{0,1:T(8,128)(2,1)} %bitcast.26, bf16[512,7168]{1,0:T(8,128)(2,1)} %param.12), kind=kOutput, calls=%fused_computation.5 | convolution fusion | flops 1880883200 | bytes 11272192 | tf_op jit(solution)/shard_map/dot_general | solution.py:88
  119.7 0.0 reduce-scatter.2.cloned.1.call-update
  119.7 77.5 %reduce-scatter.2.cloned.1.call-done = bf16[256,448]{0,1:T(8,128)(2,1)} async-done(((bf16[256,7168]{0,1:T(8,128)(2,1)}), bf16[256,448]{0,1:T(8,128)(2,1)}) %reduce-scatter.2.cloned.1.call-update) | async-done | bytes 229392 | tf_op jit(solution)/shard_map/reduce_scatter | solution.py:89
  (7 shorter events, 0.1 us)
Async XLA Ops:
  6.5 1.7 copy-start
  6.5 5.2 %copy-start.3 = (s32[32]{0:T(128)S(1)}, s32[32]{0:T(128)}, u32[]{:S(2)}) copy-start(s32[32]{0:T(128)} %param.14) | copy-start | bytes 388
  6.5 72.1 %all-gather.2.cloned.1.call-start = ((), (), s32[]{:S(2)}) async-start(), calls=%async_computation.1 | async-start | bytes 5013504 | tf_op jit(solution)/shard_map/all_gather | solution.py:57
  7.3 189.9 %reduce-scatter.2.cloned.1.call-start = ((), (), s32[]{:S(2)}) async-start(), calls=%async_computation.2 | async-start | bytes 3899392 | tf_op jit(solution)/shard_map/reduce_scatter | solution.py:89
  10.4 0.9 copy-start.2
  11.7 4.6 %copy-start.4 = (s32[32,32]{1,0:T(8,128)S(1)}, s32[32,32]{1,0:T(8,128)}, u32[]{:S(2)}) copy-start(s32[32,32]{1,0:T(8,128)} %param.15) | copy-start | bytes 12292
  88.8 5.7 %copy-start.1 = (f32[4,256,4096]{2,1,0:T(8,128)}, f32[4,256,4096]{2,1,0:T(8,128)S(1)}, u32[]{:S(2)}) copy-start(f32[4,256,4096]{2,1,0:T(8,128)S(1)} %get-tuple-element.14) | copy-start | bytes 50331652
Sparse Core Ops, SparseCore 0:
  9.9 68.6 all-gather.1
  119.8 77.3 reduce-scatter.1
where the time goes:
time: 206 us; the launch traced here: 204 us
  waiting for transfers between devices  139 us (67%)
  matrix products  37 us (18%)
  between operations  13.5 us (7%)
  local copies, waits for them, and re-layouts  7.89 us (4%)
  other arithmetic  6.31 us (3%)
    reduce_scatter x1, waiting for transfers between devices, shards(): lax.psum_scatter(partial_out.astype(jnp.bfloat16), 'tp', scatter_dimensio...  77.5 us
    all_gather x1, waiting for transfers between devices, shards(): piece = lax.all_gather(kv_latent, 'ctx', axis=0, tiled=True)  61 us
    dot_general x1, matrix products, shards(): jnp.einsum('htl,hlv->thv', o_lat, w_uv, preferred_element_type=jnp.float32)  12.8 us
    dot_general x1, matrix products, shards(): lax.dot_general(merged, piece, (((1,), (1,)), ((), ())), preferred_elemen...  10.1 us
    dot_general x1, matrix products, shards(): partial_out = jnp.dot(o_head, w_out, preferred_element_type=jnp.float32)  7.93 us
    unnamed x12, local copies, waits for them, and re-layouts  7.87 us
    reduce_sum x1, other arithmetic, shards(): total_new = jnp.sum(expo, axis=-1)  4.49 us
  transfers between devices with their start and end apart: 2, of which 2 were waited for; matrix products, arithmetic and copies ran while one was open for 4% of the time, Pallas kernels for 0%

commit v1 on v0

v1 whole, which is shorter than its diff:
```python
import jax
import jax.numpy as jnp
import numpy as np
from jax import lax
from jax.experimental import pallas as pl
from jax.experimental.pallas import tpu as pltpu
from jax.sharding import PartitionSpec as P

MESH = pl.DeviceIdType.MESH
SLAB = 128
TOK = 256
HALF = TOK // 2
HEADS = 4
NOPE = 128
ROPE = 64
LAT = 512
KEY = LAT + ROPE
QR = 1536
VD = 128
GROUP = HEADS * VD
FEAT = 448
NZ = 8
SIDE = NZ * FEAT
WINDOW = 512
PAIR = 2 * FEAT
SCALE = float((NOPE + ROPE) ** -0.5 * np.log2(np.e))
FILL = -1e30

OWN_UP, OWN_DOWN, OWN_P = 0, 2, 4
P_UP, P_DOWN, FAR_UP, FAR_DOWN, FAR_P = 6, 8, 10, 11, 12
SIB = 14
N_KV = 22


def dot(a, b):
    return jnp.dot(a, b, preferred_element_type=jnp.float32)


def kernel(
    cq_hbm, wuq_hbm, wuk_hbm, wuv_hbm, wout_hbm, kv_hbm, order_ref, table_ref, freq_ref,
    out_ref,
    cq, wuq, wuk, wuv, wown, woth, kvbuf, qbuf, acc, top, den, oown, ooth, packed, landed,
    load_sem, kv_send, kv_recv, w_send, w_recv, o_send, o_recv, r_send, r_recv,
):
    ctx = lax.axis_index("ctx")
    tp = lax.axis_index("tp")
    core = lax.rem(ctx, 2)
    yh = lax.rem(lax.div(ctx, 2), 2)
    x = lax.div(ctx, 4)
    yl = lax.div(tp, NZ)
    z = lax.rem(tp, NZ)

    def at(dx, flip_h, flip_l, dz, flip_core):
        nx = lax.rem(x + dx + 4, 4)
        nh = 1 - yh if flip_h else yh
        nl = 1 - yl if flip_l else yl
        nz = lax.rem(z + dz + NZ, NZ)
        nc = 1 - core if flip_core else core
        return ((nx * 2 + nh) * 2 + nc, nl * NZ + nz)

    up_x, down_x = at(1, 0, 0, 0, 0), at(-1, 0, 0, 0, 0)
    across, beside = at(0, 1, 1, 0, 0), at(0, 0, 1, 0, 0)
    up_z, down_z = at(0, 0, 0, 1, 0), at(0, 0, 0, -1, 0)
    sibling = at(0, 0, 0, 0, 1)

    def block(dx, flip_h, flip_core):
        return at(dx, flip_h, 0, 0, flip_core)[0]

    loads = [
        pltpu.make_async_copy(cq_hbm, cq, load_sem.at[0]),
        pltpu.make_async_copy(wuq_hbm, wuq, load_sem.at[1]),
        pltpu.make_async_copy(wuk_hbm, wuk, load_sem.at[2]),
        pltpu.make_async_copy(kv_hbm, kvbuf.at[ctx], load_sem.at[3]),
        pltpu.make_async_copy(wuv_hbm, wuv, load_sem.at[4]),
        pltpu.make_async_copy(
            wout_hbm.at[:, pl.ds(pl.multiple_of(yl * SIDE, 128), SIDE)], wown, load_sem.at[5]
        ),
    ]
    for load in loads:
        load.start()

    barrier = pltpu.get_barrier_semaphore()
    for device in (up_x, down_x, across, beside, up_z, down_z, sibling):
        pl.semaphore_signal(barrier, inc=1, device_id=device, device_id_type=MESH)
    pl.semaphore_wait(barrier, 7)

    def rows(h):
        return pl.ds(h * HALF, HALF)

    def kv_copy(index, b, h, device, own=False):
        return pltpu.make_async_remote_copy(
            src_ref=kv_hbm.at[rows(h)] if own else kvbuf.at[b, rows(h)],
            dst_ref=kvbuf.at[b, rows(h)],
            send_sem=kv_send.at[index],
            recv_sem=kv_recv.at[index],
            device_id=device,
            device_id_type=MESH,
        )

    def sib_copy(k, b, own=False):
        return pltpu.make_async_remote_copy(
            src_ref=kv_hbm if own else kvbuf.at[b],
            dst_ref=kvbuf.at[b],
            send_sem=kv_send.at[SIB + k],
            recv_sem=kv_recv.at[SIB + k],
            device_id=sibling,
            device_id_type=MESH,
        )

    places = ((0, 0), (-1, 0), (1, 0), (0, 1), (2, 0), (-1, 1), (1, 1), (2, 1))
    blocks = [block(dx, flip, 0) for dx, flip in places]
    sib_blocks = [block(dx, flip, 1) for dx, flip in places]
    own, low, high, cross, far, low_cross, high_cross, far_cross = blocks

    own_sends = []
    for h in range(2):
        own_sends += [
            kv_copy(OWN_UP + h, own, h, up_x, True),
            kv_copy(OWN_P + h, own, h, across, True),
            kv_copy(OWN_DOWN + h, own, h, down_x, True),
        ]
    own_sends.insert(0, sib_copy(0, own, True))
    for copy in own_sends:
        copy.start()

    def group_columns(g):
        base = lax.div(z, 2)
        steps = (0, 2 * lax.rem(z, 2) - 1, 1 - 2 * lax.rem(z, 2), 2)
        return lax.rem(base + steps[g] + 4, 4) * PAIR

    def quarter(dx, dc):
        return lax.rem(x + dx + 4, 4) * 128 + (1 - core if dc else core) * 64

    def w_copy(index, src, src_base, r, g, device):
        cols = group_columns(g)
        return pltpu.make_async_remote_copy(
            src_ref=src.at[pl.ds(r, 64), pl.ds(pl.multiple_of(src_base + cols, 128), PAIR)],
            dst_ref=woth.at[pl.ds(r, 64), pl.ds(pl.multiple_of(cols, 128), PAIR)],
            send_sem=w_send.at[index, g],
            recv_sem=w_recv.at[index, g],
            device_id=device,
            device_id_type=MESH,
        )

    other = (1 - yl) * SIDE
    w_dx = (0, 2, -1, 1)

    def w_beside(g):
        return w_copy(0, wout_hbm, other, quarter(0, 0), g, beside)

    def w_across(g):
        return w_copy(1, wout_hbm, other, quarter(2, 0), g, across)

    def w_up(g):
        return w_copy(2, woth, 0, quarter(0, 0), g, up_x)

    def w_down(g):
        return w_copy(3, woth, 0, quarter(0, 0), g, down_x)

    def w_landed(i, g):
        return w_copy(i, woth, 0, quarter(w_dx[i % 4], i // 4), g, sibling)

    def w_sib(i, g):
        return w_copy(4 + i, woth, 0, quarter(w_dx[i], 0), g, sibling)

    for g in range(4):
        w_beside(g).start()

    lane = lax.broadcasted_iota(jnp.int32, (SLAB, 128), 1)
    row = lax.broadcasted_iota(jnp.int32, (SLAB, 128), 0)
    delta = lane - row
    seqs = [order_ref[2 * ctx + a] for a in range(2)]
    loads[0].wait()
    loads[1].wait()
    loads[2].wait()
    first_half = lax.rem(lane, 64) < 32
    for a in range(2):
        pos = (seqs[a] * SLAB + row).astype(jnp.float32)
        angle = pos * freq_ref[0:1, :]
        cosine = jnp.cos(angle) * SCALE
        sine = jnp.sin(angle) * SCALE
        sine = jnp.where(first_half, -sine, sine)
        rows_a = pl.ds(a * SLAB, SLAB)
        for k in range(2):
            q = dot(cq[rows_a, :], wuq[:, k * 384 : (k + 1) * 384])
            shifted = pltpu.roll(q, 64, 1)
            nopes = (q[:, 0:128], shifted[:, 256:384])
            pair = jnp.where(lane < 64, q[:, 128:256], q[:, 256:384])
            swapped = jnp.where(first_half, pltpu.roll(pair, 96, 1), pltpu.roll(pair, 32, 1))
            turned = pair * cosine + swapped * sine
            ropes = (turned, pltpu.roll(turned, 64, 1))
            for j in range(2):
                h = 2 * k + j
                rows_h = pl.ds(h * SLAB, SLAB)
                q_lat = dot(nopes[j].astype(jnp.bfloat16), wuk[h]) * SCALE
                qbuf[a, rows_h, 0:LAT] = q_lat.astype(jnp.bfloat16)
                qbuf[a, rows_h, LAT:KEY] = ropes[j][:, 0:ROPE].astype(jnp.bfloat16)

    top[...] = jnp.full_like(top, FILL)
    den[...] = jnp.zeros_like(den)
    acc[...] = jnp.zeros_like(acc)

    def attend(pair):
        keys = kvbuf[pl.ds(2 * pair, 2)].reshape(2 * TOK, KEY)
        values = keys[:, 0:LAT]
        for a in range(2):
            bias = []
            for k in range(4):
                seq_k = order_ref[4 * pair + k]
                allowed = table_ref[seqs[a], seq_k] == 1
                limit = jnp.where(seq_k < seqs[a], SLAB, jnp.where(seq_k == seqs[a], 0, -SLAB))
                limit = jnp.where(allowed, limit, -SLAB)
                bias.append(jnp.where(delta <= limit, 0.0, FILL))
            bias = jnp.concatenate(bias, axis=1)
            score = lax.dot_general(
                qbuf[a], keys, (((1,), (1,)), ((), ())), preferred_element_type=jnp.float32
            )
            score = (score.reshape(HEADS, SLAB, 2 * TOK) + bias[None]).reshape(HEADS * SLAB, 2 * TOK)
            old = top[a]
            new = jnp.maximum(old, jnp.max(score, axis=1, keepdims=True))
            top[a] = new
            shrink = jnp.exp2(old - new)
            weight = jnp.exp2(score - new[:, 0:1])
            part = weight[:, 0:128]
            for k in range(1, 4):
                part = part + weight[:, k * 128 : (k + 1) * 128]
            den[a] = den[a] * shrink + part
            acc[a] = acc[a] * shrink[:, 0:1] + dot(weight.astype(jnp.bfloat16), values)

    def finish(a):
        total = jnp.sum(den[a], axis=1, keepdims=True)
        o_lat = (acc[a] / total).astype(jnp.bfloat16)
        for h in range(HEADS):
            o_head = dot(o_lat[h * SLAB : (h + 1) * SLAB], wuv[h])
            oown[pl.ds(a * SLAB, SLAB), h * VD : (h + 1) * VD] = o_head.astype(jnp.bfloat16)

    def o_copy(k):
        part = pl.ds(k * 64, 64)
        return pltpu.make_async_remote_copy(
            src_ref=oown.at[part],
            dst_ref=ooth.at[part],
            send_sem=o_send.at[k],
            recv_sem=o_recv.at[k],
            device_id=beside,
            device_id_type=MESH,
        )

    def step(i, carry):
        @pl.when(i == 0)
        def _():
            loads[3].wait()
            sib_copy(0, sib_blocks[0], True).wait_recv()

        @pl.when(i == 1)
        def _():
            kv_copy(OWN_UP, low, 0, up_x).wait_recv()
            kv_copy(FAR_UP, low, 0, up_x).start()
            kv_copy(OWN_P, cross, 0, across).wait_recv()
            kv_copy(P_UP, cross, 0, up_x).start()
            kv_copy(P_DOWN, cross, 0, down_x).start()
            kv_copy(OWN_DOWN, high, 0, down_x).wait_recv()
            kv_copy(OWN_DOWN + 1, high, 1, down_x).wait_recv()
            kv_copy(FAR_DOWN, high, 1, down_x).start()
            kv_copy(OWN_P + 1, cross, 1, across).wait_recv()
            kv_copy(P_UP + 1, cross, 1, up_x).start()
            kv_copy(P_DOWN + 1, cross, 1, down_x).start()
            kv_copy(OWN_UP + 1, low, 1, up_x).wait_recv()
            for k in range(1, 4):
                sib_copy(k, blocks[k]).start()
            sib_copy(1, sib_blocks[1]).wait_recv()

        @pl.when(i == 2)
        def _():
            kv_copy(FAR_UP, far, 0, up_x).wait_recv()
            kv_copy(FAR_P, far, 0, across).start()
            kv_copy(FAR_DOWN, far, 1, down_x).wait_recv()
            kv_copy(FAR_P + 1, far, 1, across).start()
            sib_copy(4, far).start()
            sib_copy(2, sib_blocks[2]).wait_recv()
            for g in range(4):
                w_across(g).start()

        @pl.when(i == 3)
        def _():
            sib_copy(3, sib_blocks[3]).wait_recv()

        @pl.when(i == 4)
        def _():
            sib_copy(4, sib_blocks[4]).wait_recv()

        @pl.when(i == 5)
        def _():
            for h in range(2):
                kv_copy(P_UP + h, low_cross, h, up_x).wait_recv()
                kv_copy(P_DOWN + h, high_cross, h, down_x).wait_recv()
            for k in range(5, 7):
                sib_copy(k, blocks[k]).start()
            for g in range(4):
                w_landed(0, g).wait_recv()
                w_up(g).start()
                w_down(g).start()
                w_sib(0, g).start()
            sib_copy(5, sib_blocks[5]).wait_recv()

        @pl.when(i == 6)
        def _():
            for h in range(2):
                kv_copy(FAR_P + h, far_cross, h, across).wait_recv()
            sib_copy(7, far_cross).start()
            sib_copy(6, sib_blocks[6]).wait_recv()

        @pl.when(i == 7)
        def _():
            sib_copy(7, sib_blocks[7]).wait_recv()

        pair = lax.div(own, 2)
        for k in range(1, 8):
            pair = jnp.where(i == k, lax.div(blocks[k], 2), pair)
        attend(pair)
        return carry

    lax.fori_loop(0, 8, step, 0)
    loads[4].wait()
    for a in range(2):
        finish(a)
        for u in range(2):
            o_copy(2 * a + u).start()
    loads[5].wait()

    lane32 = lax.broadcasted_iota(jnp.int32, (32, 128), 1)

    def r_copy(way, s, u):
        return pltpu.make_async_remote_copy(
            src_ref=packed.at[way, s, u],
            dst_ref=landed.at[way, s, u],
            send_sem=r_send.at[way, s, u],
            recv_sem=r_recv.at[way, s, u],
            device_id=(up_z, down_z)[way],
            device_id_type=MESH,
        )

    def reduce_step(s, carry):
        for g in range(4):

            @pl.when(s == (0, 0, 1, 2)[g])
            def _():
                w_landed(1, g).wait_recv()
                w_sib(1, g).start()
                for i in (2, 3):
                    w_landed(i, g).wait_recv()
                    w_sib(i, g).start()
                for i in range(4, 8):
                    w_landed(i, g).wait_recv()

        for way in range(2):
            d = lax.rem(z + (NZ - 1 - s if way == 0 else 1 + s) + NZ, NZ)
            odd = lax.rem(d, 2)
            even = odd == 0
            start = pl.multiple_of(d * FEAT - odd * 64, 128)
            window = pl.ds(start, WINDOW)
            rows_w = pl.ds(way * SLAB, SLAB)

            @pl.when(s == 0)
            def _():
                for u in range(2):
                    o_copy(2 * way + u).wait_recv()

            part = dot(oown[rows_w, :], wown[:, window]) + dot(ooth[rows_w, :], woth[:, window])
            main = jnp.where(even, part[:, 0:384], part[:, 128:512])
            tail = jnp.where(even, part[:, 384:512], part[:, 0:128])
            for u in range(2):
                t = u * 64
                first, second = tail[t : t + 32], tail[t + 32 : t + 64]
                tails = jnp.where(
                    even,
                    jnp.where(lane32 < 64, first, pltpu.roll(second, 64, 1)),
                    jnp.where(lane32 < 64, pltpu.roll(first, 64, 1), second),
                )
                total = jnp.concatenate([main[t : t + 32], main[t + 32 : t + 64], tails], axis=1)

                @pl.when(s == 0)
                def _():
                    packed[way, 0, u] = total.astype(jnp.bfloat16)

                @pl.when(s > 0)
                def _():
                    before = jnp.maximum(s - 1, 0)
                    r_copy(way, before, u).wait_recv()
                    packed[way, s, u] = (total + landed[way, before, u].astype(jnp.float32)).astype(
                        jnp.bfloat16
                    )

                @pl.when(s < NZ - 1)
                def _():
                    r_copy(way, jnp.minimum(s, NZ - 2), u).start()

        return carry

    lax.fori_loop(0, NZ, reduce_step, 0)

    even = lax.rem(z, 2) == 0
    for way in range(2):
        for u in range(2):
            whole = packed[way, NZ - 1, u].astype(jnp.float32)
            tails = whole[:, 768:896]
            turned = pltpu.roll(tails, 64, 1)
            for k in range(2):
                main = whole[:, k * 384 : (k + 1) * 384]
                lower, upper = (tails, turned) if k == 0 else (turned, tails)
                plain = jnp.concatenate([main, lower], axis=1)
                moved = pltpu.roll(jnp.concatenate([upper if k else turned, main], axis=1), 448, 1)
                result = jnp.where(even, plain, moved)[:, 0:FEAT]
                out_ref[pl.ds(way * SLAB + u * 64 + k * 32, 32), :] = result.astype(jnp.bfloat16)

    for copy in own_sends:
        copy.wait_send()
    for h in range(2):
        kv_copy(P_UP + h, cross, h, up_x).wait_send()
        kv_copy(P_DOWN + h, cross, h, down_x).wait_send()
        kv_copy(FAR_P + h, far, h, across).wait_send()
    kv_copy(FAR_UP, low, 0, up_x).wait_send()
    kv_copy(FAR_DOWN, high, 1, down_x).wait_send()
    for k in range(1, 8):
        sib_copy(k, blocks[k]).wait_send()
    for g in range(4):
        for copy in (w_beside(g), w_across(g), w_up(g), w_down(g)):
            copy.wait_send()
        for i in range(4):
            w_sib(i, g).wait_send()
    for k in range(4):
        o_copy(k).wait_send()
    for way in range(2):
        for s in range(NZ - 1):
            for u in range(2):
                r_copy(way, s, u).wait_send()


def shards(c_query, w_uq, w_uk, w_uv, w_out, kv_latent, slab_order, block_table):
    freqs = 10000.0 ** (-jnp.arange(ROPE // 2, dtype=jnp.float32) / (ROPE // 2))
    freqs = jnp.broadcast_to(jnp.tile(freqs, 4)[None, :], (8, 128))
    bf16 = jnp.bfloat16
    dma = pltpu.SemaphoreType.DMA
    return pl.pallas_call(
        kernel,
        out_shape=jax.ShapeDtypeStruct((TOK, FEAT), bf16),
        in_specs=[pl.BlockSpec(memory_space=pl.ANY)] * 6
        + [pl.BlockSpec(memory_space=pltpu.SMEM)] * 2
        + [pl.BlockSpec(memory_space=pltpu.VMEM)],
        out_specs=pl.BlockSpec(memory_space=pltpu.VMEM),
        scratch_shapes=[
            pltpu.VMEM((TOK, QR), bf16),
            pltpu.VMEM((QR, HEADS * (NOPE + ROPE)), bf16),
            pltpu.VMEM((HEADS, NOPE, LAT), bf16),
            pltpu.VMEM((HEADS, LAT, VD), bf16),
            pltpu.VMEM((GROUP, SIDE), bf16),
            pltpu.VMEM((GROUP, SIDE), bf16),
            pltpu.VMEM((16, TOK, KEY), bf16),
            pltpu.VMEM((2, HEADS * SLAB, KEY), bf16),
            pltpu.VMEM((2, HEADS * SLAB, LAT), jnp.float32),
            pltpu.VMEM((2, HEADS * SLAB, 128), jnp.float32),
            pltpu.VMEM((2, HEADS * SLAB, 128), jnp.float32),
            pltpu.VMEM((TOK, GROUP), bf16),
            pltpu.VMEM((TOK, GROUP), bf16),
            pltpu.VMEM((2, NZ, 2, 32, PAIR), bf16),
            pltpu.VMEM((2, NZ - 1, 2, 32, PAIR), bf16),
            dma((6,)),
            dma((N_KV,)),
            dma((N_KV,)),
            dma((8, 4)),
            dma((8, 4)),
            dma((4,)),
            dma((4,)),
            dma((2, NZ - 1, 2)),
            dma((2, NZ - 1, 2)),
        ],
        compiler_params=pltpu.CompilerParams(
            collective_id=0, has_side_effects=True, vmem_limit_bytes=58 * 2**20
        ),
        name="attention",
    )(c_query, w_uq, w_uk, w_uv, w_out, kv_latent, slab_order, block_table, freqs)


def solution(mesh):
    in_specs = (
        P("ctx", None),
        P(None, "tp"),
        P("tp", None, None),
        P("tp", None, None),
        P("tp", None),
        P("ctx", None),
        P(),
        P(),
    )
    return jax.shard_map(
        shards, mesh=mesh, in_specs=in_specs, out_specs=P("ctx", "tp"), check_vma=False
    )
```

time: 206 us -> 85.7 us (0.42)
  waiting for transfers between devices: 139 us -> 0 us
  Pallas kernels: 0 us -> 81.2 us
  matrix products: 37 us -> 0 us
  between operations: 13.5 us -> 0.02 us
  other arithmetic: 6.31 us -> 0.01 us
  local copies, waits for them, and re-layouts: 7.89 us -> 4.31 us
    pallas_call x0 -> x1, Pallas kernels: none -> 81.2 us  [shards(): pl.pallas_call(kernel, out_shape=jax.ShapeDtypeStruct((TOK, FEAT), bf16),...]
    reduce_scatter x1 -> x0, waiting for transfers between devices: 77.5 us -> none  [shards(): lax.psum_scatter(partial_out.astype(jnp.bfloat16), 'tp', scatter_dimensio...]
    all_gather x1 -> x0, waiting for transfers between devices: 61 us -> none  [shards(): piece = lax.all_gather(kv_latent, 'ctx', axis=0, tiled=True)]
    dot_general x6 -> x0, matrix products: 37 us -> none  [the longest x1 12.8 us: shards(): jnp.einsum('htl,hlv->thv', o_lat, w_uv, preferred_element_type=jnp.float32)]
    unnamed x12 -> x1, local copies, waits for them, and re-layouts: 7.87 us -> 1.84 us
    reduce_sum x3 -> x0, other arithmetic: 4.73 us -> none  [the longest x1 4.49 us: shards(): total_new = jnp.sum(expo, axis=-1)]
  transfers between devices with their start and end apart: 2 -> 0, of which waited for: 2 -> 0; matrix products, arithmetic and copies ran while one was open for 4% -> 0% of each run, Pallas kernels for 0% -> 0%
where the time goes in v1:
time: 85.7 us; the launch traced here: 85.5 us
  Pallas kernels  81.2 us (95%)
  local copies, waits for them, and re-layouts  4.31 us (5%)
    pallas_call x1, Pallas kernels, shards(): pl.pallas_call(kernel, out_shape=jax.ShapeDtypeStruct((TOK, FEAT), bf16),...  81.2 us
    unnamed x1, local copies, waits for them, and re-layouts  1.84 us
    pallas_call x1, local copies, waits for them, and re-layouts, shards(): pl.pallas_call(kernel, out_shape=jax.ShapeDtypeStruct((TOK, FEAT), bf16),...  1.78 us

profile of v1, /device:TPU:8, one launch (start us, length us, event | category | flops | bytes accessed | tf_op | source)
XLA Modules:
  0.0 85.5 jit_solution(2077656747966686289)
XLA Ops:
  0.0 0.1 broadcast_in_dim.7
  0.1 0.6 broadcast_in_dim.8.freq_ref
  0.7 1.8 %copy.9.kv_hbm = bf16[256,576]{1,0:T(8,128)(2,1)} copy(bf16[256,576]{0,1:T(8,128)(2,1)} %param.13) | data formatting | bytes 589824 | tf_op args[5]
  2.5 81.2 %attention.1 = bf16[256,448]{1,0:T(8,128)(2,1)} custom-call(bf16[256,1536]{1,0:T(8,128)(2,1)} %cq_hbm.1, bf16[1536,768]{1,0:T(8,128)(2,1)} %wuq_hbm.1, bf16[4,128,512]{2,1,0:T(8,128)(2,1)} %wuk_hbm.1, bf16[4,512,128]{2,1,0:T(8,128)(2,1)} %wuv_hbm.1, bf16[512,7168]{1,0:T(8,128)(2,1)} %wout_hbm.1, bf16[256,576]{1,0:T(8,128)(2,1)} %copy.9.kv_hbm, s32[32]{0:T(128)} %order_ref.1, ...), custom_call_target="tpu_custom_call" | custom-call | tf_op jit(solution)/shard_map/attention/pallas_call | solution.py:443
  83.7 1.8 %copy.10 = bf16[256,448]{0,1:T(8,128)(2,1)} copy(bf16[256,448]{1,0:T(8,128)(2,1)} %attention.1) | data formatting | bytes 458752 | tf_op jit(solution)/shard_map/attention/pallas_call | solution.py:443
  (2 shorter events, 0.0 us)

commit v2 on v1

v2 whole, which is shorter than its diff:
```python
import jax
import jax.numpy as jnp
import numpy as np
from jax import lax
from jax.experimental import pallas as pl
from jax.experimental.pallas import tpu as pltpu
from jax.sharding import PartitionSpec as P

MESH = pl.DeviceIdType.MESH
SLAB = 128
TOK = 256
HALF = TOK // 2
HEADS = 4
NOPE = 128
ROPE = 64
LAT = 512
KEY = LAT + ROPE
QR = 1536
VD = 128
GROUP = HEADS * VD
FEAT = 448
NZ = 8
SIDE = NZ * FEAT
WINDOW = 512
PAIR = 2 * FEAT
SCALE = float((NOPE + ROPE) ** -0.5 * np.log2(np.e))
FILL = -1e30

OWN_UP, OWN_DOWN, OWN_P = 0, 2, 4
P_UP, P_DOWN, FAR_UP, FAR_DOWN, FAR_P = 6, 8, 10, 12, 14
SIB = 16
N_KV = 32


def dot(a, b):
    return jnp.dot(a, b, preferred_element_type=jnp.float32)


def kernel(
    cq_hbm, wuq_hbm, wuk_hbm, wuv_hbm, wout_hbm, kv_hbm, order_ref, table_ref,
    out_ref,
    cq, wuq, wuk, wuv, wown, woth, kvbuf, qbuf, acc, top, den, oown, ooth, packed, landed, final, parts,
    load_sem, kv_send, kv_recv, w_send, w_recv, o_send, o_recv, r_send, r_recv,
):
    ctx = lax.axis_index("ctx")
    tp = lax.axis_index("tp")
    core = lax.rem(ctx, 2)
    yh = lax.rem(lax.div(ctx, 2), 2)
    x = lax.div(ctx, 4)
    yl = lax.div(tp, NZ)
    z = lax.rem(tp, NZ)

    def at(dx, flip_h, flip_l, dz, flip_core):
        nx = lax.rem(x + dx + 4, 4)
        nh = 1 - yh if flip_h else yh
        nl = 1 - yl if flip_l else yl
        nz = lax.rem(z + dz + NZ, NZ)
        nc = 1 - core if flip_core else core
        return ((nx * 2 + nh) * 2 + nc, nl * NZ + nz)

    up_x, down_x = at(1, 0, 0, 0, 0), at(-1, 0, 0, 0, 0)
    across, beside = at(0, 1, 1, 0, 0), at(0, 0, 1, 0, 0)
    up_z, down_z = at(0, 0, 0, 1, 0), at(0, 0, 0, -1, 0)
    sibling = at(0, 0, 0, 0, 1)

    def block(dx, flip_h, flip_core):
        return at(dx, flip_h, 0, 0, flip_core)[0]

    loads = [
        pltpu.make_async_copy(cq_hbm, cq, load_sem.at[0]),
        pltpu.make_async_copy(wuq_hbm, wuq, load_sem.at[1]),
        pltpu.make_async_copy(wuk_hbm, wuk, load_sem.at[2]),
        pltpu.make_async_copy(kv_hbm.at[:, 0:SLAB], kvbuf.at[2 * ctx], load_sem.at[3]),
        pltpu.make_async_copy(wuv_hbm, wuv, load_sem.at[4]),
        pltpu.make_async_copy(
            wout_hbm.at[:, pl.ds(pl.multiple_of(yl * SIDE, 128), SIDE)], wown, load_sem.at[5]
        ),
        pltpu.make_async_copy(kv_hbm.at[:, SLAB:TOK], kvbuf.at[2 * ctx + 1], load_sem.at[6]),
    ]
    for load in loads:
        load.start()

    barrier = pltpu.get_barrier_semaphore()
    for device in (up_x, down_x, across, beside, up_z, down_z, sibling):
        pl.semaphore_signal(barrier, inc=1, device_id=device, device_id_type=MESH)
    pl.semaphore_wait(barrier, 7)

    def source(b, h, own):
        return kv_hbm.at[:, h * SLAB : (h + 1) * SLAB] if own else kvbuf.at[2 * b + h]

    def kv_copy(index, b, h, device, own=False):
        return pltpu.make_async_remote_copy(
            src_ref=source(b, h, own),
            dst_ref=kvbuf.at[2 * b + h],
            send_sem=kv_send.at[index + h],
            recv_sem=kv_recv.at[index + h],
            device_id=device,
            device_id_type=MESH,
        )

    def part_copy(index, b, h, part, device):
        rows = pl.ds(part * (KEY // 2), KEY // 2)
        return pltpu.make_async_remote_copy(
            src_ref=kvbuf.at[2 * b + h, rows],
            dst_ref=kvbuf.at[2 * b + h, rows],
            send_sem=kv_send.at[index + h],
            recv_sem=kv_recv.at[index + h],
            device_id=device,
            device_id_type=MESH,
        )

    def sib_copy(k, b, h, own=False):
        return kv_copy(SIB + 2 * k, b, h, sibling, own)

    places = ((0, 0), (-1, 0), (1, 0), (0, 1), (2, 0), (-1, 1), (1, 1), (2, 1))
    blocks = [block(dx, flip, 0) for dx, flip in places]
    sib_blocks = [block(dx, flip, 1) for dx, flip in places]
    own, low, high, cross, far, low_cross, high_cross, far_cross = blocks

    own_sends = []
    for h in range(2):
        own_sends += [
            kv_copy(OWN_UP, own, h, up_x, True),
            kv_copy(OWN_DOWN, own, h, down_x, True),
            kv_copy(OWN_P, own, h, across, True),
            sib_copy(0, own, h, True),
        ]
    for copy in own_sends:
        copy.start()

    def group_columns(g):
        base = lax.div(z, 2)
        steps = (2, 1 - 2 * lax.rem(z, 2), 2 * lax.rem(z, 2) - 1, 0)
        return lax.rem(base + steps[g] + 4, 4) * PAIR

    def quarter(dx, dc):
        return lax.rem(x + dx + 4, 4) * 128 + (1 - core if dc else core) * 64

    def w_copy(index, src, src_base, r, g, device):
        cols = group_columns(g)
        return pltpu.make_async_remote_copy(
            src_ref=src.at[pl.ds(r, 64), pl.ds(pl.multiple_of(src_base + cols, 128), PAIR)],
            dst_ref=woth.at[pl.ds(r, 64), pl.ds(pl.multiple_of(cols, 128), PAIR)],
            send_sem=w_send.at[index, g],
            recv_sem=w_recv.at[index, g],
            device_id=device,
            device_id_type=MESH,
        )

    other = (1 - yl) * SIDE
    w_dx = (0, 2, -1, 1)

    def w_beside(g):
        return w_copy(0, wout_hbm, other, quarter(0, 0), g, beside)

    def w_across(g):
        return w_copy(1, wout_hbm, other, quarter(2, 0), g, across)

    def w_up(g):
        return w_copy(2, woth, 0, quarter(0, 0), g, up_x)

    def w_down(g):
        return w_copy(3, woth, 0, quarter(0, 0), g, down_x)

    def w_landed(i, g):
        return w_copy(i, woth, 0, quarter(w_dx[i % 4], i // 4), g, sibling)

    def w_sib(i, g):
        return w_copy(4 + i, woth, 0, quarter(w_dx[i], 0), g, sibling)

    for g in range(4):
        w_beside(g).start()

    lane = lax.broadcasted_iota(jnp.int32, (SLAB, 128), 1)
    row = lax.broadcasted_iota(jnp.int32, (SLAB, 128), 0)
    delta = lane - row
    seqs = [order_ref[2 * ctx + a] for a in range(2)]
    loads[0].wait()
    loads[1].wait()
    loads[2].wait()
    first_half = lax.rem(lane, 64) < 32
    freq = jnp.exp(lax.rem(lane, 32).astype(jnp.float32) * float(-np.log(10000.0) / 32))
    for a in range(2):
        pos = (seqs[a] * SLAB + row).astype(jnp.float32)
        angle = pos * freq
        cosine = jnp.cos(angle) * SCALE
        sine = jnp.sin(angle) * SCALE
        sine = jnp.where(first_half, -sine, sine)
        rows_a = pl.ds(a * SLAB, SLAB)
        for k in range(2):
            q = dot(cq[rows_a, :], wuq[:, k * 384 : (k + 1) * 384])
            shifted = pltpu.roll(q, 64, 1)
            nopes = (q[:, 0:128], shifted[:, 256:384])
            pair = jnp.where(lane < 64, q[:, 128:256], q[:, 256:384])
            swapped = jnp.where(first_half, pltpu.roll(pair, 96, 1), pltpu.roll(pair, 32, 1))
            turned = pair * cosine + swapped * sine
            ropes = (turned, pltpu.roll(turned, 64, 1))
            for j in range(2):
                h = 2 * k + j
                rows_h = pl.ds(h * SLAB, SLAB)
                q_lat = dot(nopes[j].astype(jnp.bfloat16), wuk[h]) * SCALE
                qbuf[a, rows_h, 0:LAT] = q_lat.astype(jnp.bfloat16)
                qbuf[a, rows_h, LAT:KEY] = ropes[j][:, 0:ROPE].astype(jnp.bfloat16)

    top[...] = jnp.full_like(top, FILL)
    den[...] = jnp.zeros_like(den)
    acc[...] = jnp.zeros_like(acc)

    def attend(slabs):
        keys = jnp.concatenate([kvbuf[slab] for slab in slabs], axis=1)
        width = len(slabs) * SLAB
        found = [order_ref[slab] for slab in slabs]

        def scores(a):
            return dot(qbuf[a], keys)

        def absorb(a, score):
            bias = []
            for seq_k in found:
                allowed = table_ref[seqs[a], seq_k] == 1
                limit = jnp.where(seq_k < seqs[a], SLAB, jnp.where(seq_k == seqs[a], 0, -SLAB))
                limit = jnp.where(allowed, limit, -SLAB)
                bias.append(jnp.where(delta <= limit, 0.0, FILL))
            bias = jnp.concatenate(bias, axis=1)
            score = (score.reshape(HEADS, SLAB, width) + bias[None]).reshape(HEADS * SLAB, width)
            old = top[a]
            new = jnp.maximum(old, jnp.max(score, axis=1, keepdims=True))
            top[a] = new
            shrink = jnp.exp2(old - new)
            weight = jnp.exp2(score - new[:, 0:1])
            part = weight[:, 0:128]
            for k in range(1, len(slabs)):
                part = part + weight[:, k * 128 : (k + 1) * 128]
            den[a] = den[a] * shrink + part
            mixed = lax.dot_general(
                weight.astype(jnp.bfloat16),
                keys[0:LAT],
                (((1,), (1,)), ((), ())),
                preferred_element_type=jnp.float32,
            )
            acc[a] = acc[a] * shrink[:, 0:1] + mixed

        first, second = scores(0), scores(1)
        absorb(0, first)
        absorb(1, second)

    def finish(a):
        total = jnp.sum(den[a], axis=1, keepdims=True)
        o_lat = (acc[a] / total).astype(jnp.bfloat16)
        for h in range(HEADS):
            o_head = dot(o_lat[h * SLAB : (h + 1) * SLAB], wuv[h])
            oown[pl.ds(a * SLAB, SLAB), h * VD : (h + 1) * VD] = o_head.astype(jnp.bfloat16)

    def o_copy(a):
        part = pl.ds(a * SLAB, SLAB)
        return pltpu.make_async_remote_copy(
            src_ref=oown.at[part],
            dst_ref=ooth.at[part],
            send_sem=o_send.at[a],
            recv_sem=o_recv.at[a],
            device_id=beside,
            device_id_type=MESH,
        )

    def land(pairs):
        for k, h in pairs:
            sib_copy(k, sib_blocks[k], h).wait_recv()

    def step(i, carry):
        @pl.when(i == 0)
        def _():
            loads[3].wait()
            loads[6].wait()
            land([(0, 0), (0, 1)])

        @pl.when(i == 1)
        def _():
            kv_copy(OWN_UP, low, 0, up_x).wait_recv()
            part_copy(FAR_UP, low, 0, 0, up_x).start()
            kv_copy(OWN_DOWN, high, 0, down_x).wait_recv()
            part_copy(FAR_DOWN, high, 0, 1, down_x).start()
            sib_copy(1, low, 0).start()
            sib_copy(2, high, 0).start()
            kv_copy(OWN_P, cross, 0, across).wait_recv()
            sib_copy(3, cross, 0).start()
            land([(1, 0), (2, 0), (3, 0)])

        @pl.when(i == 2)
        def _():
            kv_copy(OWN_UP, low, 1, up_x).wait_recv()
            part_copy(FAR_UP, low, 1, 0, up_x).start()
            kv_copy(OWN_DOWN, high, 1, down_x).wait_recv()
            part_copy(FAR_DOWN, high, 1, 1, down_x).start()
            kv_copy(P_UP, cross, 0, up_x).start()
            kv_copy(P_DOWN, cross, 0, down_x).start()
            sib_copy(1, low, 1).start()
            sib_copy(2, high, 1).start()
            kv_copy(OWN_P, cross, 1, across).wait_recv()
            kv_copy(P_UP, cross, 1, up_x).start()
            kv_copy(P_DOWN, cross, 1, down_x).start()
            sib_copy(3, cross, 1).start()
            land([(1, 1), (2, 1), (3, 1)])

        @pl.when(i == 3)
        def _():
            for h in range(2):
                part_copy(FAR_UP, far, h, 0, up_x).wait_recv()
                part_copy(FAR_DOWN, far, h, 1, down_x).wait_recv()
                kv_copy(FAR_P, far, h, across).start()
                sib_copy(4, far, h).start()
            for g in range(4):
                w_across(g).start()
            land([(4, 0), (4, 1)])

        @pl.when(i == 4)
        def _():
            kv_copy(P_UP, low_cross, 0, up_x).wait_recv()
            sib_copy(5, low_cross, 0).start()
            kv_copy(P_DOWN, high_cross, 0, down_x).wait_recv()
            sib_copy(6, high_cross, 0).start()
            for g in range(4):
                w_landed(0, g).wait_recv()
                w_up(g).start()
                w_down(g).start()
            land([(5, 0), (6, 0)])

        @pl.when(i == 5)
        def _():
            kv_copy(FAR_P, far_cross, 0, across).wait_recv()
            sib_copy(7, far_cross, 0).start()
            kv_copy(P_UP, low_cross, 1, up_x).wait_recv()
            sib_copy(5, low_cross, 1).start()
            kv_copy(P_DOWN, high_cross, 1, down_x).wait_recv()
            sib_copy(6, high_cross, 1).start()
            kv_copy(FAR_P, far_cross, 1, across).wait_recv()
            sib_copy(7, far_cross, 1).start()
            for g in range(4):
                w_sib(0, g).start()
            land([(5, 1), (6, 1), (7, 0), (7, 1)])

        def slabs(k, h):
            return [2 * blocks[k] + h, 2 * sib_blocks[k] + h]

        def pick(choices, at_steps):
            chosen = choices[0]
            for choice, at_step in zip(choices[1:], at_steps):
                chosen = [jnp.where(i == at_step, b, a) for a, b in zip(chosen, choice)]
            return chosen

        @pl.when((i == 0) | (i == 3) | (i == 4))
        def _():
            attend(
                pick(
                    [
                        slabs(0, 0) + slabs(0, 1),
                        slabs(4, 0) + slabs(4, 1),
                        slabs(5, 0) + slabs(6, 0),
                    ],
                    (3, 4),
                )
            )

        @pl.when((i == 1) | (i == 2))
        def _():
            attend(
                pick([slabs(1, 0) + slabs(2, 0) + slabs(3, 0), slabs(1, 1) + slabs(2, 1) + slabs(3, 1)], (2,))
            )

        @pl.when(i == 5)
        def _():
            attend(slabs(5, 1) + slabs(6, 1) + slabs(7, 0) + slabs(7, 1))

        return carry

    lax.fori_loop(0, 6, step, 0)
    loads[4].wait()
    for a in range(2):
        finish(a)
        o_copy(a).start()
    loads[5].wait()

    lane64 = lax.broadcasted_iota(jnp.int32, (64, 128), 1)
    FOUR_UP, FOUR_DOWN, THREE_UP, THREE_DOWN = 0, 4, 8, 11

    def r_copy(k, device):
        return pltpu.make_async_remote_copy(
            src_ref=packed.at[k],
            dst_ref=landed.at[k],
            send_sem=r_send.at[k],
            recv_sem=r_recv.at[k],
            device_id=device,
            device_id_type=MESH,
        )

    def chunk(dz):
        d = lax.rem(z + dz + NZ, NZ)
        odd = lax.rem(d, 2)
        return odd == 0, pl.ds(pl.multiple_of(d * FEAT - odd * 64, 128), WINDOW)

    def mine(dz):
        parts[dz % NZ] = dot(oown[...], wown[:, chunk(dz)[1]])

    def others(dz, a=None):
        rows_a = pl.ds(0, TOK) if a is None else pl.ds(a * SLAB, SLAB)
        parts[dz % NZ, rows_a] += dot(ooth[rows_a, :], woth[:, chunk(dz)[1]])

    def pack(dz, a):
        even = chunk(dz)[0]
        part = parts[dz % NZ, pl.ds(a * SLAB, SLAB)]
        main = jnp.where(even, part[:, 0:384], part[:, 128:512])
        tail = jnp.where(even, part[:, 384:512], part[:, 0:128])
        first, second = tail[0:64], tail[64:128]
        tails = jnp.where(
            even,
            jnp.where(lane64 < 64, first, pltpu.roll(second, 64, 1)),
            jnp.where(lane64 < 64, pltpu.roll(first, 64, 1), second),
        )
        return jnp.concatenate([main[0:64], main[64:128], tails], axis=1)

    def send(k, dz, a, device, follows):
        total = pack(dz, a)
        if follows:
            r_copy(k - 1, device).wait_recv()
            total = total + landed[k - 1].astype(jnp.float32)
        packed[k] = total.astype(jnp.bfloat16)
        r_copy(k, device).start()

    def land_group(g):
        w_landed(1, g).wait_recv()
        w_sib(1, g).start()
        for i in (2, 3):
            w_landed(i, g).wait_recv()
            w_sib(i, g).start()
        for i in range(4, 8):
            w_landed(i, g).wait_recv()

    for dz in (4, 3, -3):
        mine(dz)
    land_group(0)
    o_copy(0).wait_recv()
    others(4, 0)
    send(FOUR_UP, 4, 0, up_z, False)
    o_copy(1).wait_recv()
    others(4, 1)
    send(FOUR_DOWN, 4, 1, down_z, False)
    land_group(1)
    for dz in (3, -3):
        others(dz)
    send(THREE_UP, 3, 1, up_z, False)
    send(THREE_DOWN, -3, 0, down_z, False)
    for t in range(1, 4):
        dz = 4 - t
        send(FOUR_UP + t, dz, 0, up_z, True)
        send(FOUR_DOWN + t, -dz, 1, down_z, True)
        if t < 3:
            land_group(t + 1)
            for nearer in (dz - 1, 1 - dz):
                mine(nearer)
                others(nearer)
            send(THREE_UP + t, dz - 1, 1, up_z, True)
            send(THREE_DOWN + t, 1 - dz, 0, down_z, True)
        else:
            mine(0)
            others(0)

    even = chunk(0)[0]
    for a, (k, m) in enumerate(((THREE_DOWN + 2, FOUR_UP + 3), (THREE_UP + 2, FOUR_DOWN + 3))):
        whole = pack(0, a)
        for number, device in ((k, down_z), (m, up_z)):
            r_copy(number, device).wait_recv()
            whole = whole + landed[number].astype(jnp.float32)
        tails = whole[:, 768:896]
        turned = pltpu.roll(tails, 64, 1)
        for k in range(2):
            main = whole[:, k * 384 : (k + 1) * 384]
            lower, upper = (tails, turned) if k == 0 else (turned, tails)
            plain = jnp.concatenate([main, lower], axis=1)
            moved = pltpu.roll(jnp.concatenate([upper, main], axis=1), 448, 1)
            final[pl.ds(a * SLAB + k * 64, 64), :] = jnp.where(even, plain, moved)
    out_ref[...] = jnp.transpose(final[...])[0:FEAT].astype(jnp.bfloat16)

    for copy in own_sends:
        copy.wait_send()
    for h in range(2):
        kv_copy(P_UP, cross, h, up_x).wait_send()
        kv_copy(P_DOWN, cross, h, down_x).wait_send()
        kv_copy(FAR_P, far, h, across).wait_send()
        part_copy(FAR_UP, low, h, 0, up_x).wait_send()
        part_copy(FAR_DOWN, high, h, 1, down_x).wait_send()
        for k in range(1, 8):
            sib_copy(k, blocks[k], h).wait_send()
    for g in range(4):
        for copy in (w_beside(g), w_across(g), w_up(g), w_down(g)):
            copy.wait_send()
        for i in range(4):
            w_sib(i, g).wait_send()
    for a in range(2):
        o_copy(a).wait_send()
    for k in range(14):
        r_copy(k, up_z).wait_send()


def shards(c_query, w_uq, w_uk, w_uv, w_out, kv_latent, slab_order, block_table):
    bf16 = jnp.bfloat16
    dma = pltpu.SemaphoreType.DMA
    turned = pl.pallas_call(
        kernel,
        out_shape=jax.ShapeDtypeStruct((FEAT, TOK), bf16),
        in_specs=[pl.BlockSpec(memory_space=pl.ANY)] * 6
        + [pl.BlockSpec(memory_space=pltpu.SMEM)] * 2,
        out_specs=pl.BlockSpec(memory_space=pltpu.VMEM),
        scratch_shapes=[
            pltpu.VMEM((TOK, QR), bf16),
            pltpu.VMEM((QR, HEADS * (NOPE + ROPE)), bf16),
            pltpu.VMEM((HEADS, NOPE, LAT), bf16),
            pltpu.VMEM((HEADS, LAT, VD), bf16),
            pltpu.VMEM((GROUP, SIDE), bf16),
            pltpu.VMEM((GROUP, SIDE), bf16),
            pltpu.VMEM((32, KEY, SLAB), bf16),
            pltpu.VMEM((2, HEADS * SLAB, KEY), bf16),
            pltpu.VMEM((2, HEADS * SLAB, LAT), jnp.float32),
            pltpu.VMEM((2, HEADS * SLAB, 128), jnp.float32),
            pltpu.VMEM((2, HEADS * SLAB, 128), jnp.float32),
            pltpu.VMEM((TOK, GROUP), bf16),
            pltpu.VMEM((TOK, GROUP), bf16),
            pltpu.VMEM((14, 64, PAIR), bf16),
            pltpu.VMEM((14, 64, PAIR), bf16),
            pltpu.VMEM((TOK, WINDOW), jnp.float32),
            pltpu.VMEM((NZ, TOK, WINDOW), jnp.float32),
            dma((7,)),
            dma((N_KV,)),
            dma((N_KV,)),
            dma((8, 4)),
            dma((8, 4)),
            dma((2,)),
            dma((2,)),
            dma((14,)),
            dma((14,)),
        ],
        compiler_params=pltpu.CompilerParams(
            collective_id=0, has_side_effects=True, vmem_limit_bytes=58 * 2**20
        ),
        name="attention",
    )(c_query, w_uq, w_uk, w_uv, w_out, kv_latent.T, slab_order, block_table)
    return turned.T


def solution(mesh):
    in_specs = (
        P("ctx", None),
        P(None, "tp"),
        P("tp", None, None),
        P("tp", None, None),
        P("tp", None),
        P("ctx", None),
        P(),
        P(),
    )
    return jax.shard_map(
        shards, mesh=mesh, in_specs=in_specs, out_specs=P("ctx", "tp"), check_vma=False
    )
```

time: 85.7 us -> 70.4 us (0.82)
  Pallas kernels: 81.2 us -> 68.1 us
  local copies, waits for them, and re-layouts: 4.31 us -> 1.64 us
    pallas_call x1, Pallas kernels: 81.2 us -> 68.1 us  [shards(): pl.pallas_call(kernel, out_shape=jax.ShapeDtypeStruct((FEAT, TOK), bf16),...]
    pallas_call x1 -> x0, local copies, waits for them, and re-layouts: 1.78 us -> none  [shards(): pl.pallas_call(kernel, out_shape=jax.ShapeDtypeStruct((TOK, FEAT), bf16),...]
where the time goes in v2:
time: 70.4 us; the launch traced here: 69.8 us
  Pallas kernels  68.1 us (97%)
  local copies, waits for them, and re-layouts  1.64 us (2%)
    pallas_call x1, Pallas kernels, shards(): pl.pallas_call(kernel, out_shape=jax.ShapeDtypeStruct((FEAT, TOK), bf16),...  68.1 us
    unnamed x1, local copies, waits for them, and re-layouts  1.64 us

profile of v2, /device:TPU:8, one launch (start us, length us, event | category | flops | bytes accessed | tf_op | source)
XLA Modules:
  0.0 69.8 jit_solution(13796594372973569442)
XLA Ops:
  0.0 68.1 %attention.1 = bf16[448,256]{1,0:T(8,128)(2,1)} custom-call(bf16[256,1536]{1,0:T(8,128)(2,1)} %cq_hbm.1, bf16[1536,768]{1,0:T(8,128)(2,1)} %wuq_hbm.1, bf16[4,128,512]{2,1,0:T(8,128)(2,1)} %wuk_hbm.1, bf16[4,512,128]{2,1,0:T(8,128)(2,1)} %wuv_hbm.1, bf16[512,7168]{1,0:T(8,128)(2,1)} %wout_hbm.1, bf16[576,256]{1,0:T(8,128)(2,1)} %bitcast.3, s32[32]{0:T(128)} %order_ref.1, ...), custom_call_target="tpu_custom_call" | custom-call | tf_op jit(solution)/shard_map/attention/pallas_call | solution.py:506
  68.2 1.6 %copy.10 = bf16[256,448]{0,1:T(8,128)(2,1)} copy(bf16[256,448]{0,1:T(8,128)(2,1)} %bitcast.2) | data formatting | bytes 458752

commit v3 on v2

v3 whole, which is shorter than its diff:
```python
import jax
import jax.numpy as jnp
import numpy as np
from jax import lax
from jax.experimental import pallas as pl
from jax.experimental.pallas import tpu as pltpu
from jax.sharding import PartitionSpec as P

MESH = pl.DeviceIdType.MESH
SLAB = 128
TOK = 256
HALF = TOK // 2
HEADS = 4
NOPE = 128
ROPE = 64
LAT = 512
KEY = LAT + ROPE
QR = 1536
VD = 128
GROUP = HEADS * VD
FEAT = 448
NZ = 8
SIDE = NZ * FEAT
WINDOW = 512
PAIR = 2 * FEAT
SCALE = float((NOPE + ROPE) ** -0.5 * np.log2(np.e))
FILL = -1e30

N_KV = 48
WHOLE, UPPER, LOWER = (0, KEY), (0, KEY // 2), (KEY // 2, KEY // 2)


def dot(a, b):
    return jnp.dot(a, b, preferred_element_type=jnp.float32)


def kernel(
    cq_hbm, wuq_hbm, wuk_hbm, wuv_hbm, wout_hbm, kv_hbm, order_ref, table_ref,
    out_ref,
    cq, wuq, wuk, wuv, wown, woth, kvbuf, qbuf, acc, top, den, oown, ooth, packed, landed, parts,
    load_sem, kv_send, kv_recv, w_send, w_recv, o_send, o_recv, r_send, r_recv,
):
    ctx = lax.axis_index("ctx")
    tp = lax.axis_index("tp")
    core = lax.rem(ctx, 2)
    yh = lax.rem(lax.div(ctx, 2), 2)
    x = lax.div(ctx, 4)
    yl = lax.div(tp, NZ)
    z = lax.rem(tp, NZ)

    def at(dx, flip_h, flip_l, dz, flip_core):
        nx = lax.rem(x + dx + 4, 4)
        nh = 1 - yh if flip_h else yh
        nl = 1 - yl if flip_l else yl
        nz = lax.rem(z + dz + NZ, NZ)
        nc = 1 - core if flip_core else core
        return ((nx * 2 + nh) * 2 + nc, nl * NZ + nz)

    up_x, down_x = at(1, 0, 0, 0, 0), at(-1, 0, 0, 0, 0)
    across, beside = at(0, 1, 1, 0, 0), at(0, 0, 1, 0, 0)
    up_z, down_z = at(0, 0, 0, 1, 0), at(0, 0, 0, -1, 0)
    sibling = at(0, 0, 0, 0, 1)

    def block(dx, flip_h, flip_core):
        return at(dx, flip_h, 0, 0, flip_core)[0]

    loads = [
        pltpu.make_async_copy(cq_hbm, cq, load_sem.at[0]),
        pltpu.make_async_copy(wuq_hbm, wuq, load_sem.at[1]),
        pltpu.make_async_copy(wuk_hbm, wuk, load_sem.at[2]),
        pltpu.make_async_copy(kv_hbm.at[:, 0:SLAB], kvbuf.at[2 * ctx], load_sem.at[3]),
        pltpu.make_async_copy(wuv_hbm, wuv, load_sem.at[4]),
        pltpu.make_async_copy(
            wout_hbm.at[:, pl.ds(pl.multiple_of(yl * SIDE, 128), SIDE)], wown, load_sem.at[5]
        ),
        pltpu.make_async_copy(kv_hbm.at[:, SLAB:TOK], kvbuf.at[2 * ctx + 1], load_sem.at[6]),
    ]
    for load in loads:
        load.start()

    barrier = pltpu.get_barrier_semaphore()
    for device in (up_x, down_x, across, beside, up_z, down_z, sibling):
        pl.semaphore_signal(barrier, inc=1, device_id=device, device_id_type=MESH)
    pl.semaphore_wait(barrier, 7)

    here = lax.rem(z, 2)
    there = 1 - here
    targets = {
        "up_x": up_x, "down_x": down_x, "across": across, "up_z": up_z, "down_z": down_z, "sibling": sibling,
    }
    places = {
        "own": (0, 0), "low": (-1, 0), "high": (1, 0), "cross": (0, 1),
        "far": (2, 0), "low_cross": (-1, 1), "high_cross": (1, 1), "far_cross": (2, 1),
    }
    blocks = {name: block(dx, flip, 0) for name, (dx, flip) in places.items()}
    sib_blocks = {name: block(dx, flip, 1) for name, (dx, flip) in places.items()}
    numbers, sent = {}, []

    def kv_copy(tag, name, h, rows, target, theirs=False):
        number = numbers.setdefault(tag, len(numbers))
        slab = 2 * (sib_blocks if theirs else blocks)[name] + h
        part = pl.ds(*rows)
        source = kvbuf.at[slab, part]
        if name == "own":
            source = kv_hbm.at[part, pl.ds(pl.multiple_of(h * SLAB, SLAB), SLAB)]
        return pltpu.make_async_remote_copy(
            src_ref=source,
            dst_ref=kvbuf.at[slab, part],
            send_sem=kv_send.at[number],
            recv_sem=kv_recv.at[number],
            device_id=targets[target],
            device_id_type=MESH,
        )

    def give(tag, name, h, target, rows=WHOLE):
        sent.append((tag, name, h, rows, target))
        kv_copy(tag, name, h, rows, target).start()

    def take(tag, name, h, rows=WHOLE):
        kv_copy(tag, name, h, rows, "sibling").wait_recv()

    def is_here(h):
        return "h" if h is here else "t"

    def share(names, h):
        for name in names:
            give("s" + name + is_here(h), name, h, "sibling")

    def land(names, h):
        for name in names:
            kv_copy("s" + name + is_here(h), name, h, WHOLE, "sibling", True).wait_recv()

    for tag, rows in (("u", UPPER), ("l", LOWER)):
        for target in ("up_x", "down_x", "across"):
            give(target + tag, "own", here, target, rows)
    give("across", "own", there, "across")
    share(["own"], here)
    share(["own"], there)

    def group_columns(g):
        base = lax.div(z, 2)
        steps = (2, 1 - 2 * lax.rem(z, 2), 2 * lax.rem(z, 2) - 1, 0)
        return lax.rem(base + steps[g] + 4, 4) * PAIR

    def quarter(dx, dc):
        return lax.rem(x + dx + 4, 4) * 128 + (1 - core if dc else core) * 64

    def w_copy(index, src, src_base, r, n, g, device):
        cols = group_columns(g)
        return pltpu.make_async_remote_copy(
            src_ref=src.at[pl.ds(r, n), pl.ds(pl.multiple_of(src_base + cols, 128), PAIR)],
            dst_ref=woth.at[pl.ds(r, n), pl.ds(pl.multiple_of(cols, 128), PAIR)],
            send_sem=w_send.at[index, g],
            recv_sem=w_recv.at[index, g],
            device_id=device,
            device_id_type=MESH,
        )

    other = (1 - yl) * SIDE
    w_dx = (0, 2, 1, -1)

    def w_beside(k, g):
        return w_copy(k, wout_hbm, other, quarter(w_dx[k], 0), 64, g, beside)

    def w_across(g):
        return w_copy(2, wout_hbm, other, quarter(1, 0), 64, g, across)

    def w_up(g):
        return w_copy(3, woth, 0, quarter(0, 0), 32, g, up_x)

    def w_down(g):
        return w_copy(4, woth, 0, quarter(2, 0) + 32, 32, g, down_x)

    def w_landed(k, g):
        if k < 3:
            return w_copy(k, woth, 0, quarter(w_dx[k], 0), 64, g, sibling)
        if k < 5:
            return w_copy(k, woth, 0, quarter(-1, 0) + 32 * (k - 3), 32, g, sibling)
        return w_copy(k, woth, 0, quarter(w_dx[k - 5], 1), 64, g, sibling)

    def w_sib(k, g):
        return w_copy(5 + k, woth, 0, quarter(w_dx[k], 0), 64, g, sibling)

    def pass_on(g):
        for k in range(2):
            w_landed(k, g).wait_recv()
            w_sib(k, g).start()
        w_up(g).start()
        w_down(g).start()

    for g in range(4):
        for k in range(2):
            w_beside(k, g).start()

    lane = lax.broadcasted_iota(jnp.int32, (SLAB, 128), 1)
    row = lax.broadcasted_iota(jnp.int32, (SLAB, 128), 0)
    delta = lane - row
    seqs = [order_ref[2 * ctx + a] for a in range(2)]
    loads[0].wait()
    loads[1].wait()
    loads[2].wait()
    first_half = lax.rem(lane, 64) < 32
    freq = jnp.exp(lax.rem(lane, 32).astype(jnp.float32) * float(-np.log(10000.0) / 32))
    for a in range(2):
        pos = (seqs[a] * SLAB + row).astype(jnp.float32)
        angle = pos * freq
        cosine = jnp.cos(angle) * SCALE
        sine = jnp.sin(angle) * SCALE
        sine = jnp.where(first_half, -sine, sine)
        rows_a = pl.ds(a * SLAB, SLAB)
        for k in range(2):
            q = dot(cq[rows_a, :], wuq[:, k * 384 : (k + 1) * 384])
            shifted = pltpu.roll(q, 64, 1)
            nopes = (q[:, 0:128], shifted[:, 256:384])
            pair = jnp.where(lane < 64, q[:, 128:256], q[:, 256:384])
            swapped = jnp.where(first_half, pltpu.roll(pair, 96, 1), pltpu.roll(pair, 32, 1))
            turned = pair * cosine + swapped * sine
            ropes = (turned, pltpu.roll(turned, 64, 1))
            for j in range(2):
                h = 2 * k + j
                q_lat = dot(nopes[j].astype(jnp.bfloat16), wuk[h]) * SCALE
                for u in range(2):
                    rows_h = pl.ds((a * HEADS + h) * 64, 64)
                    half = slice(u * 64, u * 64 + 64)
                    qbuf[u, rows_h, 0:LAT] = q_lat[half].astype(jnp.bfloat16)
                    qbuf[u, rows_h, LAT:KEY] = ropes[j][half, 0:ROPE].astype(jnp.bfloat16)

    top[...] = jnp.full_like(top, FILL)
    den[...] = jnp.zeros_like(den)
    acc[...] = jnp.zeros_like(acc)

    def scores(u, keys):
        return dot(qbuf[u], keys)

    def absorb(u, slabs, keys, score):
        width = len(slabs) * SLAB
        biases = []
        for a in range(2):
            bias = []
            for slab in slabs:
                seq_k = order_ref[slab]
                allowed = table_ref[seqs[a], seq_k] == 1
                limit = jnp.where(seq_k < seqs[a], SLAB, jnp.where(seq_k == seqs[a], 0, -SLAB))
                limit = jnp.where(allowed, limit, -SLAB)
                bias.append(jnp.where(delta[u * 64 : u * 64 + 64] <= limit, 0.0, FILL))
            biases.append(jnp.concatenate(bias, axis=1))
        bias = jnp.stack(biases)
        score = (score.reshape(2, HEADS, 64, width) + bias[:, None]).reshape(2 * HEADS * 64, width)
        old = top[u]
        new = jnp.maximum(old, jnp.max(score, axis=1, keepdims=True))
        top[u] = new
        shrink = jnp.exp2(old - new)
        weight = jnp.exp2(score - new[:, 0:1])
        part = weight[:, 0:128]
        for k in range(1, len(slabs)):
            part = part + weight[:, k * 128 : (k + 1) * 128]
        den[u] = den[u] * shrink + part
        mixed = lax.dot_general(
            weight.astype(jnp.bfloat16),
            keys[0:LAT],
            (((1,), (1,)), ((), ())),
            preferred_element_type=jnp.float32,
        )
        acc[u] = acc[u] * shrink[:, 0:1] + mixed

    def attend(slabs, last=False):
        keys = jnp.concatenate([kvbuf[slab] for slab in slabs], axis=1)
        first, second = scores(0, keys), scores(1, keys)
        absorb(0, slabs, keys, first)
        if last:
            finish(0)
            o_copy(0).start()
        absorb(1, slabs, keys, second)
        if last:
            finish(1)
            o_copy(1).start()

    def finish(u):
        total = jnp.sum(den[u], axis=1, keepdims=True)
        o_lat = (acc[u] / total).astype(jnp.bfloat16).reshape(2, HEADS, 64, LAT)
        for h in range(HEADS):
            o_head = dot(o_lat[:, h].reshape(SLAB, LAT), wuv[h])
            oown[pl.ds(u * SLAB, SLAB), h * VD : (h + 1) * VD] = o_head.astype(jnp.bfloat16)

    def o_copy(a):
        part = pl.ds(a * SLAB, SLAB)
        return pltpu.make_async_remote_copy(
            src_ref=oown.at[part],
            dst_ref=ooth.at[part],
            send_sem=o_send.at[a],
            recv_sem=o_recv.at[a],
            device_id=beside,
            device_id_type=MESH,
        )

    near = ["low", "high", "cross"]
    later = ["far", "low_cross", "high_cross"]

    def step(i, carry):
        @pl.when(i == 0)
        def _():
            take("up_xu", "low", here, UPPER)
            give("far_u", "low", here, "up_x", UPPER)
            take("acrossu", "cross", here, UPPER)
            give("cross_du", "cross", here, "down_x", UPPER)
            give("cross_uu", "cross", here, "up_x", UPPER)
            take("down_xu", "high", here, UPPER)
            take("down_xl", "high", here, LOWER)
            give("far_l", "high", here, "down_x", LOWER)
            take("acrossl", "cross", here, LOWER)
            give("cross_dl", "cross", here, "down_x", LOWER)
            give("cross_ul", "cross", here, "up_x", LOWER)
            give("up_x", "own", there, "up_x")
            give("down_x", "own", there, "down_x")
            take("up_xl", "low", here, LOWER)
            share(near, here)
            loads[3].wait()
            loads[6].wait()
            land(["own"], here)
            land(["own"], there)

        @pl.when(i == 1)
        def _():
            take("far_u", "far", here, UPPER)
            give("far_cross_u", "far", here, "across", UPPER)
            give("z_far_u", "far", here, "up_z", UPPER)
            take("far_l", "far", here, LOWER)
            give("far_cross_l", "far", here, "across", LOWER)
            give("z_far_l", "far", here, "down_z", LOWER)
            share(["far"], here)
            take("cross_du", "high_cross", here, UPPER)
            give("z_high_u", "high_cross", here, "up_z", UPPER)
            take("cross_uu", "low_cross", here, UPPER)
            give("z_low_u", "low_cross", here, "up_z", UPPER)
            take("cross_dl", "high_cross", here, LOWER)
            give("z_high_l", "high_cross", here, "down_z", LOWER)
            take("cross_ul", "low_cross", here, LOWER)
            give("z_low_l", "low_cross", here, "down_z", LOWER)
            share(["high_cross", "low_cross"], here)
            land(near, here)

        @pl.when(i == 2)
        def _():
            take("across", "cross", there)
            share(["cross"], there)
            take("far_cross_u", "far_cross", here, UPPER)
            give("z_fc_u", "far_cross", here, "up_z", UPPER)
            take("far_cross_l", "far_cross", here, LOWER)
            give("z_fc_l", "far_cross", here, "down_z", LOWER)
            share(["far_cross"], here)
            for g in range(4):
                w_across(g).start()
            take("up_x", "low", there)
            take("down_x", "high", there)
            share(["low", "high"], there)
            land(later, here)

        @pl.when(i == 3)
        def _():
            take("z_far_u", "far", there, UPPER)
            take("z_far_l", "far", there, LOWER)
            share(["far"], there)
            take("z_high_u", "high_cross", there, UPPER)
            take("z_high_l", "high_cross", there, LOWER)
            share(["high_cross"], there)
            take("z_low_u", "low_cross", there, UPPER)
            take("z_low_l", "low_cross", there, LOWER)
            share(["low_cross"], there)
            land(near, there)
            for g in range(2):
                pass_on(g)

        @pl.when(i == 4)
        def _():
            take("z_fc_u", "far_cross", there, UPPER)
            take("z_fc_l", "far_cross", there, LOWER)
            share(["far_cross"], there)
            land(later, there)

        @pl.when(i == 5)
        def _():
            for g in range(2, 4):
                pass_on(g)
            land(["far_cross"], here)
            land(["far_cross"], there)

        def slabs(names, h):
            return [2 * of[name] + h for name in names for of in (blocks, sib_blocks)]

        def pick(choices):
            chosen = choices[0]
            for k, choice in enumerate(choices[1:]):
                chosen = [jnp.where(i == k + 2, b, a) for a, b in zip(chosen, choice)]
            return chosen

        @pl.when(i == 0)
        def _():
            attend(slabs(["own"], 0) + slabs(["own"], 1))

        @pl.when((i > 0) & (i < 5))
        def _():
            attend(pick([slabs(near, here), slabs(later, here), slabs(near, there), slabs(later, there)]))

        @pl.when(i == 5)
        def _():
            loads[4].wait()
            attend(slabs(["far_cross"], 0) + slabs(["far_cross"], 1), True)

        return carry

    lax.fori_loop(0, 6, step, 0)
    loads[5].wait()

    lane32 = lax.broadcasted_iota(jnp.int32, (32, 128), 1)
    FOUR_UP, FOUR_DOWN, THREE_UP, THREE_DOWN = 0, 4, 8, 11

    def r_copy(k, u, device):
        return pltpu.make_async_remote_copy(
            src_ref=packed.at[k, u],
            dst_ref=landed.at[k, u],
            send_sem=r_send.at[k, u],
            recv_sem=r_recv.at[k, u],
            device_id=device,
            device_id_type=MESH,
        )

    def chunk(dz):
        d = lax.rem(z + dz + NZ, NZ)
        odd = lax.rem(d, 2)
        return odd == 0, pl.ds(pl.multiple_of(d * FEAT - odd * 64, 128), WINDOW)

    def mine(dz):
        parts[dz % NZ] = dot(oown[...], wown[:, chunk(dz)[1]])

    def others(dz, u=None):
        rows_u = pl.ds(0, TOK) if u is None else pl.ds(u * SLAB, SLAB)
        parts[dz % NZ, rows_u] += dot(ooth[rows_u, :], woth[:, chunk(dz)[1]])

    def pack(dz, a, u):
        even = chunk(dz)[0]
        part = parts[dz % NZ, pl.ds(u * SLAB + a * 64, 64)]
        main = jnp.where(even, part[:, 0:384], part[:, 128:512])
        tail = jnp.where(even, part[:, 384:512], part[:, 0:128])
        first, second = tail[0:32], tail[32:64]
        tails = jnp.where(
            even,
            jnp.where(lane32 < 64, first, pltpu.roll(second, 64, 1)),
            jnp.where(lane32 < 64, pltpu.roll(first, 64, 1), second),
        )
        return jnp.concatenate([main[0:32], main[32:64], tails], axis=1)

    def send(k, dz, a, u, device, follows):
        total = pack(dz, a, u)
        if follows:
            r_copy(k - 1, u, device).wait_recv()
            total = total + landed[k - 1, u].astype(jnp.float32)
        packed[k, u] = total.astype(jnp.bfloat16)
        r_copy(k, u, device).start()

    def land_group(g):
        w_landed(2, g).wait_recv()
        w_sib(2, g).start()
        for k in (3, 4):
            w_landed(k, g).wait_recv()
        w_sib(3, g).start()
        for k in range(5, 9):
            w_landed(k, g).wait_recv()

    for dz in (4, 3, -3):
        mine(dz)
    land_group(0)
    land_group(1)
    for u in range(2):
        o_copy(u).wait_recv()
        others(4, u)
        send(FOUR_UP, 4, 0, u, up_z, False)
        send(FOUR_DOWN, 4, 1, u, down_z, False)
        for dz in (3, -3):
            others(dz, u)
        send(THREE_UP, 3, 1, u, up_z, False)
        send(THREE_DOWN, -3, 0, u, down_z, False)
    for t in range(1, 4):
        dz = 4 - t
        for u in range(2):
            send(FOUR_UP + t, dz, 0, u, up_z, True)
            send(FOUR_DOWN + t, -dz, 1, u, down_z, True)
        if t < 3:
            land_group(t + 1)
            for nearer in (dz - 1, 1 - dz):
                mine(nearer)
                others(nearer)
            for u in range(2):
                send(THREE_UP + t, dz - 1, 1, u, up_z, True)
                send(THREE_DOWN + t, 1 - dz, 0, u, down_z, True)
        else:
            mine(0)
            others(0)

    even = chunk(0)[0]
    for u in range(2):
        for a, (n, m) in enumerate(((THREE_DOWN + 2, FOUR_UP + 3), (THREE_UP + 2, FOUR_DOWN + 3))):
            whole = pack(0, a, u)
            for number, device in ((n, down_z), (m, up_z)):
                r_copy(number, u, device).wait_recv()
                whole = whole + landed[number, u].astype(jnp.float32)
            tails = whole[:, 768:896]
            turned = pltpu.roll(tails, 64, 1)
            for k in range(2):
                main = whole[:, k * 384 : (k + 1) * 384]
                lower, upper = (tails, turned) if k == 0 else (turned, tails)
                plain = jnp.concatenate([main, lower], axis=1)
                moved = pltpu.roll(jnp.concatenate([upper, main], axis=1), 448, 1)
                result = jnp.where(even, plain, moved)[:, 0:FEAT]
                out_ref[pl.ds(a * SLAB + u * 64 + k * 32, 32), :] = result.astype(jnp.bfloat16)

    for tag, name, h, rows, target in sent:
        kv_copy(tag, name, h, rows, target).wait_send()
    for g in range(4):
        for copy in (w_beside(0, g), w_beside(1, g), w_across(g), w_up(g), w_down(g)):
            copy.wait_send()
        for i in range(4):
            w_sib(i, g).wait_send()
    for u in range(2):
        o_copy(u).wait_send()
    for k in range(14):
        for u in range(2):
            r_copy(k, u, up_z).wait_send()


def shards(c_query, w_uq, w_uk, w_uv, w_out, kv_latent, slab_order, block_table):
    bf16 = jnp.bfloat16
    dma = pltpu.SemaphoreType.DMA
    return pl.pallas_call(
        kernel,
        out_shape=jax.ShapeDtypeStruct((TOK, FEAT), bf16),
        in_specs=[pl.BlockSpec(memory_space=pl.ANY)] * 6
        + [pl.BlockSpec(memory_space=pltpu.SMEM)] * 2,
        out_specs=pl.BlockSpec(memory_space=pltpu.VMEM),
        scratch_shapes=[
            pltpu.VMEM((TOK, QR), bf16),
            pltpu.VMEM((QR, HEADS * (NOPE + ROPE)), bf16),
            pltpu.VMEM((HEADS, NOPE, LAT), bf16),
            pltpu.VMEM((HEADS, LAT, VD), bf16),
            pltpu.VMEM((GROUP, SIDE), bf16),
            pltpu.VMEM((GROUP, SIDE), bf16),
            pltpu.VMEM((32, KEY, SLAB), bf16),
            pltpu.VMEM((2, HEADS * SLAB, KEY), bf16),
            pltpu.VMEM((2, HEADS * SLAB, LAT), jnp.float32),
            pltpu.VMEM((2, HEADS * SLAB, 128), jnp.float32),
            pltpu.VMEM((2, HEADS * SLAB, 128), jnp.float32),
            pltpu.VMEM((TOK, GROUP), bf16),
            pltpu.VMEM((TOK, GROUP), bf16),
            pltpu.VMEM((14, 2, 32, PAIR), bf16),
            pltpu.VMEM((14, 2, 32, PAIR), bf16),
            pltpu.VMEM((NZ, TOK, WINDOW), jnp.float32),
            dma((7,)),
            dma((N_KV,)),
            dma((N_KV,)),
            dma((9, 4)),
            dma((9, 4)),
            dma((2,)),
            dma((2,)),
            dma((14, 2)),
            dma((14, 2)),
        ],
        compiler_params=pltpu.CompilerParams(
            collective_id=0, has_side_effects=True, vmem_limit_bytes=58 * 2**20
        ),
        name="attention",
    )(c_query, w_uq, w_uk, w_uv, w_out, kv_latent.T, slab_order, block_table)


def solution(mesh):
    in_specs = (
        P("ctx", None),
        P(None, "tp"),
        P("tp", None, None),
        P("tp", None, None),
        P("tp", None),
        P("ctx", None),
        P(),
        P(),
    )
    return jax.shard_map(
        shards, mesh=mesh, in_specs=in_specs, out_specs=P("ctx", "tp"), check_vma=False
    )
```

time: 70.4 us -> 64.9 us (0.922)
  the two profiles are of different devices: /device:TPU:8 before, /device:TPU:1 now
where the time goes in v3:
time: 64.9 us; the launch traced here: 64.7 us
  Pallas kernels  62.9 us (97%)
  local copies, waits for them, and re-layouts  1.78 us (3%)
    pallas_call x1, Pallas kernels, shards(): pl.pallas_call(kernel, out_shape=jax.ShapeDtypeStruct((TOK, FEAT), bf16),...  62.9 us
    pallas_call x1, local copies, waits for them, and re-layouts, shards(): pl.pallas_call(kernel, out_shape=jax.ShapeDtypeStruct((TOK, FEAT), bf16),...  1.78 us

profile of v3, /device:TPU:1, one launch (start us, length us, event | category | flops | bytes accessed | tf_op | source)
XLA Modules:
  0.0 64.7 jit_solution(1343985823301300918)
XLA Ops:
  0.0 62.9 %attention.1 = bf16[256,448]{1,0:T(8,128)(2,1)} custom-call(bf16[256,1536]{1,0:T(8,128)(2,1)} %cq_hbm.1, bf16[1536,768]{1,0:T(8,128)(2,1)} %wuq_hbm.1, bf16[4,128,512]{2,1,0:T(8,128)(2,1)} %wuk_hbm.1, bf16[4,512,128]{2,1,0:T(8,128)(2,1)} %wuv_hbm.1, bf16[512,7168]{1,0:T(8,128)(2,1)} %wout_hbm.1, bf16[576,256]{1,0:T(8,128)(2,1)} %bitcast.1, s32[32]{0:T(128)} %order_ref.1, ...), custom_call_target="tpu_custom_call" | custom-call | tf_op jit(solution)/shard_map/attention/pallas_call | solution.py:533
  62.9 1.8 %copy.9 = bf16[256,448]{0,1:T(8,128)(2,1)} copy(bf16[256,448]{1,0:T(8,128)(2,1)} %attention.1) | data formatting | bytes 458752 | tf_op jit(solution)/shard_map/attention/pallas_call | solution.py:533

commit v4 on v3

--- a/solution.py
+++ b/solution.py
@@ -180,6 +180,17 @@
 
     def w_sib(k, g):
         return w_copy(5 + k, woth, 0, quarter(w_dx[k], 0), 64, g, sibling)
+
+    def relay(g):
+        w_landed(2, g).wait_recv()
+        w_sib(2, g).start()
+        for k in (3, 4):
+            w_landed(k, g).wait_recv()
+        w_sib(3, g).start()
+
+    def settle(g):
+        for k in range(5, 9):
+            w_landed(k, g).wait_recv()
 
     def pass_on(g):
         for k in range(2):
@@ -376,11 +387,13 @@
             take("z_fc_l", "far_cross", there, LOWER)
             share(["far_cross"], there)
             land(later, there)
+            pass_on(2)
 
         @pl.when(i == 5)
         def _():
-            for g in range(2, 4):
-                pass_on(g)
+            pass_on(3)
+            relay(0)
+            relay(1)
             land(["far_cross"], here)
             land(["far_cross"], there)
 
@@ -457,24 +470,17 @@
         packed[k, u] = total.astype(jnp.bfloat16)
         r_copy(k, u, device).start()
 
-    def land_group(g):
-        w_landed(2, g).wait_recv()
-        w_sib(2, g).start()
-        for k in (3, 4):
-            w_landed(k, g).wait_recv()
-        w_sib(3, g).start()
-        for k in range(5, 9):
-            w_landed(k, g).wait_recv()
-
     for dz in (4, 3, -3):
         mine(dz)
-    land_group(0)
-    land_group(1)
+    settle(0)
     for u in range(2):
         o_copy(u).wait_recv()
         others(4, u)
         send(FOUR_UP, 4, 0, u, up_z, False)
         send(FOUR_DOWN, 4, 1, u, down_z, False)
+        if u == 0:
+            settle(1)
+            relay(2)
         for dz in (3, -3):
             others(dz, u)
         send(THREE_UP, 3, 1, u, up_z, False)
@@ -485,7 +491,9 @@
             send(FOUR_UP + t, dz, 0, u, up_z, True)
             send(FOUR_DOWN + t, -dz, 1, u, down_z, True)
         if t < 3:
-            land_group(t + 1)
+            if t == 1:
+                relay(3)
+            settle(t + 1)
             for nearer in (dz - 1, 1 - dz):
                 mine(nearer)
                 others(nearer)

time: 64.9 us -> 63 us (0.971)
  the two profiles are of different devices: /device:TPU:1 before, /device:TPU:8 now
where the time goes in v4:
time: 63 us; the launch traced here: 62.8 us
  Pallas kernels  61 us (97%)
  local copies, waits for them, and re-layouts  1.78 us (3%)
    pallas_call x1, Pallas kernels, shards(): pl.pallas_call(kernel, out_shape=jax.ShapeDtypeStruct((TOK, FEAT), bf16),...  61 us
    pallas_call x1, local copies, waits for them, and re-layouts, shards(): pl.pallas_call(kernel, out_shape=jax.ShapeDtypeStruct((TOK, FEAT), bf16),...  1.78 us

profile of v4, /device:TPU:8, one launch (start us, length us, event | category | flops | bytes accessed | tf_op | source)
XLA Modules:
  0.0 62.8 jit_solution(14880450555953762649)
XLA Ops:
  0.0 61.0 %attention.1 = bf16[256,448]{1,0:T(8,128)(2,1)} custom-call(bf16[256,1536]{1,0:T(8,128)(2,1)} %cq_hbm.1, bf16[1536,768]{1,0:T(8,128)(2,1)} %wuq_hbm.1, bf16[4,128,512]{2,1,0:T(8,128)(2,1)} %wuk_hbm.1, bf16[4,512,128]{2,1,0:T(8,128)(2,1)} %wuv_hbm.1, bf16[512,7168]{1,0:T(8,128)(2,1)} %wout_hbm.1, bf16[576,256]{1,0:T(8,128)(2,1)} %bitcast.1, s32[32]{0:T(128)} %order_ref.1, ...), custom_call_target="tpu_custom_call" | custom-call | tf_op jit(solution)/shard_map/attention/pallas_call | solution.py:541
  61.0 1.8 %copy.9 = bf16[256,448]{0,1:T(8,128)(2,1)} copy(bf16[256,448]{1,0:T(8,128)(2,1)} %attention.1) | data formatting | bytes 458752 | tf_op jit(solution)/shard_map/attention/pallas_call | solution.py:541
